TPU v7x, 1024 devices: a whole 4x4x32 slice. The times are simulated.
1024 devices in a mesh: dp: 16 (over y, x), expert: 64 (over z, core).
Axes of the slice: x: 4, y: 4, z: 32, core: 2. Of those that a mesh axis runs over, the one named last changes fastest.
Arguments:
- tokens: bfloat16 [8192, 3584], P('expert'), may hold values from -6 to 6
- up_saved: bfloat16 [8192, 8, 2048], P('expert', None, 'dp'), may hold values from -6 to 6
- hidden_grad: bfloat16 [8192, 8, 2048], P('expert', None, 'dp'), may hold values from -1.5 to 1.5
- route_device: int32 [8192, 8], P('expert'), may hold values from 0 to 255, as said below
- on_replica: int32 [64, 64], replicated, may hold values from 0 to 1, as said below
- gate_weight: bfloat16 [64, 3584, 2048], P('expert', None, 'dp'), may hold values from -0.09375 to 0.09375
Outputs:
- token_grad: bfloat16 [8192, 3584], P('expert', 'dp')
- gate_grad: bfloat16 [64, 3584, 2048], P('expert', None, 'dp')
Inputs may be any that keep to these rules, and one draw needn't show every extreme that they name: `route_device`: each token names 8 different numbers. In each aligned block of 128 tokens (those of one index of expert) every number that the block names is named by exactly 4 tokens. Numbers under 64 are devices along expert; device n holds expert n and a replica of expert (n + 32) mod 64. For every device n along expert, some block of tokens that names n has on_replica 1 for n.
All inputs are finite; a program needn't handle non-finite values.
Results may differ from a plain program's by a relative error of at most 0.022.
Values may be sent and summed in bfloat16 or wider, within the bound.
A program may use at most 32 MiB of HBM per device.

v0:
```python
import jax
import jax.numpy as jnp
from jax import lax
from jax.sharding import PartitionSpec as P

CAP = 4


def shifted(value, axis, by):
    length = lax.axis_size(axis)
    return lax.ppermute(value, axis, [(i, (i + by) % length) for i in range(length)])


def gate_delta_of(gate_value, grad_rows, up_rows):
    logistic = jax.nn.sigmoid(gate_value)
    slope = logistic * (1.0 + gate_value * (1.0 - logistic))
    return (grad_rows.astype(jnp.float32) * up_rows.astype(jnp.float32) * slope).astype(
        jnp.bfloat16
    )


def local(tokens, up_saved, hidden_grad, route_device, on_replica, gate_weight):
    experts = lax.axis_size("expert")
    halfway = experts // 2
    own_index = lax.axis_index("expert")
    tok_count, top_count = route_device.shape
    model_width = tokens.shape[1]
    hidden_local = gate_weight.shape[2]
    slot_count = experts * CAP
    routes = route_device.reshape(tok_count * top_count)
    inside = routes < experts
    onehot = (routes[:, None] == jnp.arange(experts, dtype=jnp.int32)[None, :]).astype(jnp.int32)
    earlier = jnp.cumsum(onehot, axis=0) - onehot
    position = jnp.sum(earlier * onehot, axis=1)
    slot_of = jnp.where(inside, routes * CAP + position, -1)
    placed = slot_of[None, :] == jnp.arange(slot_count, dtype=jnp.int32)[:, None]
    route_matrix = placed.astype(jnp.bfloat16)
    token_matrix = jnp.any(placed.reshape(slot_count, tok_count, top_count), axis=2).astype(
        jnp.bfloat16
    )
    route_aux = jnp.concatenate([hidden_grad, up_saved], axis=2).reshape(
        tok_count * top_count, 2 * hidden_local
    )
    aux_send = jnp.dot(route_matrix, route_aux, preferred_element_type=jnp.float32).astype(
        jnp.bfloat16
    )
    aux_send = aux_send.reshape(experts, CAP, 2 * hidden_local)
    rows_send = jnp.dot(token_matrix, tokens, preferred_element_type=jnp.float32).astype(
        jnp.bfloat16
    )
    rows_recv, aux_recv = (
        lax.all_to_all(
            rows_send.reshape(experts, CAP, model_width),
            "expert",
            split_axis=0,
            concat_axis=0,
            tiled=True,
        ),
        lax.all_to_all(aux_send, "expert", split_axis=0, concat_axis=0, tiled=True),
    )
    flag_source = lax.dynamic_slice_in_dim(on_replica, own_index, 1, 1)[:, 0] == 1
    replica_rows = jnp.repeat(flag_source, CAP)[:, None]
    rows_flat = rows_recv.reshape(slot_count, model_width)
    aux_flat = aux_recv.reshape(slot_count, 2 * hidden_local)
    home_weight = gate_weight[0]
    guest_weight = shifted(home_weight, "expert", halfway)
    both_weights = jnp.concatenate([home_weight, guest_weight], axis=1)
    gate_both = jnp.dot(rows_flat, both_weights, preferred_element_type=jnp.float32)
    gate_value = jnp.where(replica_rows, gate_both[:, hidden_local:], gate_both[:, :hidden_local])
    gate_delta = gate_delta_of(gate_value, aux_flat[:, :hidden_local], aux_flat[:, hidden_local:])
    nothing = jnp.zeros_like(gate_delta)
    delta_both = jnp.concatenate(
        [
            jnp.where(replica_rows, nothing, gate_delta),
            jnp.where(replica_rows, gate_delta, nothing),
        ],
        axis=1,
    )
    partial_value = jnp.einsum(
        "sh,dh->sd", delta_both, both_weights, preferred_element_type=jnp.float32
    )
    grads_both = jnp.einsum("sd,sh->dh", rows_flat, delta_both, preferred_element_type=jnp.float32)
    returned = shifted(grads_both[:, hidden_local:].astype(jnp.bfloat16), "expert", halfway)
    weight_grad = (grads_both[:, :hidden_local] + returned.astype(jnp.float32)).astype(jnp.bfloat16)
    slot_grad = lax.psum_scatter(
        partial_value.astype(jnp.bfloat16), "dp", scatter_dimension=1, tiled=True
    )
    share_width = slot_grad.shape[1]
    arrived = lax.all_to_all(
        slot_grad.reshape(experts, CAP, share_width),
        "expert",
        split_axis=0,
        concat_axis=0,
        tiled=True,
    )
    token_grad = jnp.einsum(
        "st,sd->td",
        token_matrix,
        arrived.reshape(slot_count, share_width),
        preferred_element_type=jnp.float32,
    )
    return (token_grad.astype(jnp.bfloat16), weight_grad[None])


def solution(mesh):
    placed = (
        P("expert", None),
        P("expert", None, "dp"),
        P("expert", None, "dp"),
        P("expert", None),
        P(),
        P("expert", None, "dp"),
    )
    return jax.shard_map(
        local,
        mesh=mesh,
        in_specs=placed,
        out_specs=(P("expert", "dp"), P("expert", None, "dp")),
        check_vma=False,
    )
```

profile of v0, /device:TPU:1, one launch (start us, length us, event | category | flops | bytes accessed | tf_op | source)
XLA Modules:
  0.0 720.1 jit_solution(9480067763515991761)
XLA Ops:
  7.2 0.0 copy-start
  7.2 0.0 copy-start.5
  7.2 0.0 copy-start.4
  7.2 0.9 copy.33
  8.1 0.1 eq.54
  8.2 0.1 eq.58
  8.3 18.0 %reduce-window.6 = s32[64,8,128]{2,1,0:T(8,128)S(1)} reduce-window(s32[64,8,128]{2,1,0:T(8,128)S(1)} %fusion.10, s32[]{:T(128)} %constant.11.clone.1), window={size=1x1x128 pad=0_0x0_0x127_0}, to_apply=%region_0.0 | reduce-window | flops 8323072 | bytes 524292 | tf_op jit(solution)/shard_map/reduce-window
  26.3 0.0 copy-start.3
  26.3 0.1 slice.33
  26.5 0.1 copy.35
  26.6 0.1 copy.36
  26.7 0.1 broadcast_add_fusion
  26.9 0.1 fusion.9
  27.0 0.0 copy-done.5
  27.0 0.0 copy-done.4
  27.0 0.3 convolution_convert_fusion.2
  27.3 0.7 reshape.71
  28.0 30.4 %all-to-all-start = ((bf16[64,4,256]{2,1,0:T(4,128)(2,1)}), bf16[64,4,256]{2,1,0:T(4,128)(2,1)S(1)}, u32[]{:S(2)}, u32[]{:S(2)}) async-start(bf16[64,4,256]{2,1,0:T(4,128)(2,1)} %reshape.71), calls=%async_computation | async-start | bytes 262144 | tf_op jit(solution)/shard_map/all_to_all | solution.py:59
  58.4 0.1 reduce_sum.12
  58.5 0.0 copy-done.3
  58.5 0.4 fusion.2
  58.9 0.0 copy-done
  58.9 0.6 convolution_convert_fusion
  59.6 1.5 reshape.73
  61.0 0.0 copy-start.2
  61.0 28.0 %all-to-all-done = bf16[64,4,256]{2,1,0:T(4,128)(2,1)S(1)} async-done(((bf16[64,4,256]{2,1,0:T(4,128)(2,1)}), bf16[64,4,256]{2,1,0:T(4,128)(2,1)S(1)}, u32[]{:S(2)}, u32[]{:S(2)}) %all-to-all-start) | async-done | bytes 131104 | tf_op jit(solution)/shard_map/all_to_all | solution.py:59
  89.1 6.5 all-to-all-start.1
  95.6 0.0 reduce-scatter.2.cloned.1.call-start
  95.6 21.8 %collective-permute-start = (bf16[3584,128]{1,0:T(8,128)(2,1)}, bf16[3584,128]{1,0:T(8,128)(2,1)}, u32[]{:S(2)}, u32[]{:S(2)}) collective-permute-start(bf16[3584,128]{1,0:T(8,128)(2,1)} %bitcast.3), channel_id=1, source_target_pairs={{0,32},{1,33},{2,34},{3,35},{4,36},{5,37},{6,38},{7,39},{8,40},{9,... | collective-permute-start | bytes 2752520 | tf_op jit(solution)/shard_map/ppermute | solution.py:11
  117.5 0.0 copy-done.2
  117.5 0.2 fusion.12
  117.7 0.1 broadcast_in_dim.38
  117.8 0.1 broadcast_in_dim.39
  118.0 0.1 copy.41
  118.1 0.1 copy.42
  118.2 144.9 %all-to-all-done.1 = bf16[64,4,3584]{2,1,0:T(4,128)(2,1)} async-done(((bf16[64,4,3584]{2,1,0:T(4,128)(2,1)}), bf16[64,4,3584]{2,1,0:T(4,128)(2,1)}, u32[]{:S(2)}, u32[]{:S(2)}) %all-to-all-start.1) | async-done | bytes 1835040 | tf_op jit(solution)/shard_map/all_to_all | solution.py:52
  263.1 2.9 reshape.74
  266.0 102.1 %collective-permute-done = bf16[3584,128]{1,0:T(8,128)(2,1)} collective-permute-done((bf16[3584,128]{1,0:T(8,128)(2,1)}, bf16[3584,128]{1,0:T(8,128)(2,1)}, u32[]{:S(2)}, u32[]{:S(2)}) %collective-permute-start) | collective-permute-done | bytes 917536 | tf_op jit(solution)/shard_map/ppermute | solution.py:11
  368.2 2.3 fusion.1
  370.5 0.1 broadcast_select_fusion.1
  370.6 3.3 convolution_convert_fusion.1
  373.9 0.0 reduce-scatter.2.cloned.1.call-update
  373.9 0.7 fusion.11
  374.6 0.0 copy-start.1
  374.6 1.8 copy-done.1
  376.4 0.1 slice.53
  376.5 1.9 collective-permute-start.1
  378.5 276.0 %reduce-scatter.2.cloned.1.call-done = bf16[256,224]{0,1:T(8,128)(2,1)} async-done(((bf16[256,3584]{0,1:T(8,128)(2,1)}), bf16[256,224]{0,1:T(8,128)(2,1)}) %reduce-scatter.2.cloned.1.call-update) | async-done | bytes 114704 | tf_op jit(solution)/shard_map/reduce_scatter | solution.py:85
  654.5 1.0 copy.40
  655.5 0.7 reshape.75
  656.2 25.5 %all-to-all-start.2 = ((bf16[64,4,224]{2,1,0:T(4,128)(2,1)}), bf16[64,4,224]{2,1,0:T(4,128)(2,1)S(1)}, u32[]{:S(2)}, u32[]{:S(2)}) async-start(bf16[64,4,224]{2,1,0:T(4,128)(2,1)} %reshape.75), calls=%async_computation.3 | async-start | bytes 262144 | tf_op jit(solution)/shard_map/all_to_all | solution.py:89
  681.6 0.0 collective-permute-done.1
  681.7 2.6 fusion.3
  684.3 28.1 %all-to-all-done.2 = bf16[64,4,224]{2,1,0:T(4,128)(2,1)S(1)} async-done(((bf16[64,4,224]{2,1,0:T(4,128)(2,1)}), bf16[64,4,224]{2,1,0:T(4,128)(2,1)S(1)}, u32[]{:S(2)}, u32[]{:S(2)}) %all-to-all-start.2) | async-done | bytes 114720 | tf_op jit(solution)/shard_map/all_to_all | solution.py:89
  712.3 0.1 reshape.76
  712.4 0.9 convolution_convert_fusion.3
  (9 shorter events, 0.2 us)
Async XLA Ops:
  7.2 51.8 %copy-start = (bf16[128,3584]{1,0:T(8,128)(2,1)S(1)}, bf16[128,3584]{1,0:T(8,128)(2,1)}, u32[]{:S(2)}) copy-start(bf16[128,3584]{1,0:T(8,128)(2,1)} %param.6) | copy-start | bytes 2752516
  7.2 19.8 %copy-start.5 = (bf16[128,8,128]{2,1,0:T(8,128)(2,1)S(1)}, bf16[128,8,128]{2,1,0:T(8,128)(2,1)}, u32[]{:S(2)}) copy-start(bf16[128,8,128]{2,1,0:T(8,128)(2,1)} %param.8) | copy-start | bytes 786436
  7.2 19.8 %copy-start.4 = (bf16[128,8,128]{2,1,0:T(8,128)(2,1)S(1)}, bf16[128,8,128]{2,1,0:T(8,128)(2,1)}, u32[]{:S(2)}) copy-start(bf16[128,8,128]{2,1,0:T(8,128)(2,1)} %param.7) | copy-start | bytes 786436
  26.3 32.2 %copy-start.3 = (s32[128,8]{0,1:T(8,128)S(1)}, s32[128,8]{0,1:T(8,128)}, u32[]{:S(2)}) copy-start(s32[128,8]{0,1:T(8,128)} %param.9) | copy-start | bytes 12292
  28.0 61.1 %all-to-all-start = ((bf16[64,4,256]{2,1,0:T(4,128)(2,1)}), bf16[64,4,256]{2,1,0:T(4,128)(2,1)S(1)}, u32[]{:S(2)}, u32[]{:S(2)}) async-start(bf16[64,4,256]{2,1,0:T(4,128)(2,1)} %reshape.71), calls=%async_computation | async-start | bytes 262144 | tf_op jit(solution)/shard_map/all_to_all | solution.py:59
  61.0 56.5 %copy-start.2 = (s32[64,64]{1,0:T(8,128)S(1)}, s32[64,64]{1,0:T(8,128)}, u32[]{:S(2)}) copy-start(s32[64,64]{1,0:T(8,128)} %param.10) | copy-start | bytes 49156
  89.1 174.0 %all-to-all-start.1 = ((bf16[64,4,3584]{2,1,0:T(4,128)(2,1)}), bf16[64,4,3584]{2,1,0:T(4,128)(2,1)}, u32[]{:S(2)}, u32[]{:S(2)}) async-start(bf16[64,4,3584]{2,1,0:T(4,128)(2,1)} %reshape.73), calls=%async_computation.1 | async-start | bytes 3670016 | tf_op jit(solution)/shard_map/all_to_all | solution.py:52
  95.6 558.9 %reduce-scatter.2.cloned.1.call-start = ((), (), s32[]{:S(2)}) async-start(), calls=%async_computation.4 | async-start | bytes 1949696 | tf_op jit(solution)/shard_map/reduce_scatter | solution.py:85
  95.6 272.5 %collective-permute-start = (bf16[3584,128]{1,0:T(8,128)(2,1)}, bf16[3584,128]{1,0:T(8,128)(2,1)}, u32[]{:S(2)}, u32[]{:S(2)}) collective-permute-start(bf16[3584,128]{1,0:T(8,128)(2,1)} %bitcast.3), channel_id=1, source_target_pairs={{0,32},{1,33},{2,34},{3,35},{4,36},{5,37},{6,38},{7,39},{8,40},{9,... | collective-permute-start | bytes 2752520 | tf_op jit(solution)/shard_map/ppermute | solution.py:11
  374.6 1.8 copy-start.1
  376.5 305.1 %collective-permute-start.1 = (bf16[3584,128]{1,0:T(8,128)(2,1)S(1)}, bf16[3584,128]{1,0:T(8,128)(2,1)S(1)}, u32[]{:S(2)}, u32[]{:S(2)}) collective-permute-start(bf16[3584,128]{1,0:T(8,128)(2,1)S(1)} %slice.53), channel_id=1, source_target_pairs={{0,32},{1,33},{2,34},{3,35},{4,36},{5,37},{6,38},{7,39},{8,40},{9,... | collective-permute-start | bytes 2752520 | tf_op jit(solution)/shard_map/ppermute | solution.py:11
  656.2 56.2 %all-to-all-start.2 = ((bf16[64,4,224]{2,1,0:T(4,128)(2,1)}), bf16[64,4,224]{2,1,0:T(4,128)(2,1)S(1)}, u32[]{:S(2)}, u32[]{:S(2)}) async-start(bf16[64,4,224]{2,1,0:T(4,128)(2,1)} %reshape.75), calls=%async_computation.3 | async-start | bytes 262144 | tf_op jit(solution)/shard_map/all_to_all | solution.py:89
Sparse Core Ops, SparseCore 0:
  374.0 280.3 reduce-scatter.1
where the time goes:
time: 721 us; the launch traced here: 720 us
  waiting for transfers between devices  579 us (80%)
  starting transfers between devices  86.2 us (12%)
  other arithmetic  21.5 us (3%)
  between operations  14.3 us (2%)
  local copies, waits for them, and re-layouts  10.8 us (1%)
  matrix products  8.12 us (1%)
    reduce_scatter x1, waiting for transfers between devices, local(): lax.psum_scatter(partial_value.astype(jnp.bfloat16), 'dp', scatter_dimens...  276 us
    all_to_all x1, waiting for transfers between devices, local(): lax.all_to_all(rows_send.reshape(experts, CAP, model_width), 'expert', sp...  145 us
    ppermute x2, waiting for transfers between devices, shifted(): lax.ppermute(value, axis, [(i, (i + by) % length) for i in range(length)])  102 us
    all_to_all x1, starting transfers between devices, local(): lax.all_to_all(aux_send, 'expert', split_axis=0, concat_axis=0, tiled=True)  30.4 us
    all_to_all x1, waiting for transfers between devices, local(): lax.all_to_all(slot_grad.reshape(experts, CAP, share_width), 'expert', sp...  28.1 us
    all_to_all x1, waiting for transfers between devices, local(): lax.all_to_all(aux_send, 'expert', split_axis=0, concat_axis=0, tiled=True)  28 us
    all_to_all x1, starting transfers between devices, local(): lax.all_to_all(slot_grad.reshape(experts, CAP, share_width), 'expert', sp...  25.5 us
    ppermute x2, starting transfers between devices, shifted(): lax.ppermute(value, axis, [(i, (i + by) % length) for i in range(length)])  23.8 us
  transfers between devices with their start and end apart: 6, of which 5 were waited for; matrix products, arithmetic and copies ran while one was open for 2% of the time, Pallas kernels for 0%

commit v1 on v0

v1 whole, which is shorter than its diff:
```python
import functools

import jax
import jax.numpy as jnp
from jax import lax
from jax.experimental import pallas as pl
from jax.experimental.pallas import tpu as pltpu
from jax.sharding import PartitionSpec as P

CAP = 4
SLOTS = 2 * CAP
PAIR = 2 * SLOTS
MESH = pl.DeviceIdType.MESH
F32 = jnp.float32
BF16 = jnp.bfloat16


def dot(a, b, contract=((1,), (0,))):
    return lax.dot_general(a, b, (contract, ((), ())), preferred_element_type=F32)


def await_bytes(view, sem):
    pltpu.make_async_copy(view, view, sem).wait()


def kernel(
    parts,
    chips,
    share,
    tok_ref,
    prod_ref,
    route_ref,
    flag_ref,
    weight_ref,
    token_out,
    weight_out,
    pick,
    own_rows,
    own_aux,
    away_rows,
    away_aux,
    twin_rows,
    twin_aux,
    rows,
    aux,
    wide,
    partial,
    terms,
    delta,
    back,
    ret,
    twin_ret,
    grads,
    send_sems,
    recv_sems,
):
    experts = 2 * chips
    halfway = experts // 2
    slots = chips * PAIR
    tokens = tok_ref.shape[0]
    hidden = prod_ref.shape[2]
    routes = prod_ref.shape[0]
    part = lax.axis_index("dp")
    place = lax.axis_index("expert")
    chip = place // 2
    core = place % 2
    twin = (part, chip * 2 + 1 - core)

    def far(step):
        return (part, lax.rem(chip + step, chips) * 2 + core)

    def beside(step):
        return (lax.rem(part + step, parts), place)

    barrier = pltpu.get_barrier_semaphore()

    def greet(device):
        pl.semaphore_signal(barrier, inc=1, device_id=device, device_id_type=MESH)

    greet(twin)

    @pl.loop(1, chips)
    def _(step):
        greet(far(step))

    @pl.loop(1, parts)
    def _(step):
        greet(beside(step))

    wide[pl.ds(share, wide.shape[0] - share), :] = jnp.zeros(
        (wide.shape[0] - share, wide.shape[1]), BF16
    )

    named = route_ref[...]
    numbers = lax.broadcasted_iota(jnp.int32, (experts, tokens), 0)
    count = jnp.zeros((experts, tokens), F32)
    for k in range(routes):
        count = count + jnp.where(named[k : k + 1, :] == numbers, 1.0, 0.0)
    before = lax.broadcasted_iota(jnp.int32, (tokens, tokens), 0)
    after = lax.broadcasted_iota(jnp.int32, (tokens, tokens), 1)
    earlier = dot(count.astype(BF16), jnp.where(before < after, 1.0, 0.0).astype(BF16))
    flags = flag_ref[...].astype(F32)
    target = []
    for k in range(routes):
        here = named[k : k + 1, :] == numbers
        position = jnp.sum(jnp.where(here, earlier, 0.0), axis=0, keepdims=True).astype(jnp.int32)
        flag = jnp.sum(jnp.where(here, flags, 0.0), axis=0, keepdims=True).astype(jnp.int32)
        number = named[k : k + 1, :]
        server = lax.rem(number + flag * halfway, experts)
        row = (server // 2) * PAIR + core * SLOTS + flag * CAP + position
        target.append((jnp.where(number < experts, row, -1), lax.rem(server, 2)))

    row_ids = lax.broadcasted_iota(jnp.int32, (slots, tokens), 0)

    def fill(side, rows_ref, aux_ref):
        total = jnp.zeros((slots, hidden), F32)
        every = jnp.zeros((slots, tokens), F32)
        for k in range(routes):
            row, parity = target[k]
            chosen = jnp.where(row_ids == jnp.where(parity == side, row, -1), 1.0, 0.0)
            every = every + chosen
            total = total + dot(chosen.astype(BF16), prod_ref[k])
        matrix = every.astype(BF16)
        rows_ref[...] = dot(matrix, tok_ref[...]).astype(BF16)
        aux_ref[...] = total.astype(BF16)
        return matrix

    pick[1] = fill(1 - core, away_rows, away_aux)

    pl.semaphore_wait(barrier, 1 + (chips - 1) + (parts - 1))

    def remote(src, dst, sem, device):
        copy = pltpu.make_async_remote_copy(
            src_ref=src,
            dst_ref=dst,
            send_sem=send_sems.at[sem],
            recv_sem=recv_sems.at[sem],
            device_id=device,
            device_id_type=MESH,
        )
        copy.start()

    remote(away_rows, twin_rows, 0, twin)
    remote(away_aux, twin_aux, 1, twin)

    own_columns = pl.ds(pl.multiple_of(part * hidden, hidden), hidden)

    @pl.loop(1, parts)
    def _(step):
        other = lax.rem(part + step, parts)
        remote(
            weight_ref.at[pl.ds(pl.multiple_of(other * share, 16), share)],
            wide.at[pl.ds(0, share), own_columns],
            2,
            (other, place),
        )

    wide[pl.ds(0, share), own_columns] = weight_ref[
        pl.ds(pl.multiple_of(part * share, 16), share), :
    ]
    pick[0] = fill(core, own_rows, own_aux)

    await_bytes(twin_rows, recv_sems.at[0])
    own_rows[...] = own_rows[...] + twin_rows[...]

    def sixteen(index):
        return pl.ds(pl.multiple_of(index * PAIR, PAIR), PAIR)

    @pl.loop(1, chips)
    def _(step):
        other = lax.rem(chip + step, chips)
        remote(own_rows.at[sixteen(other)], rows.at[sixteen(chips - step)], 3, far(step))

    rows[pl.ds(0, PAIR), :] = own_rows[sixteen(chip), :]
    await_bytes(twin_aux, recv_sems.at[1])
    own_aux[...] = own_aux[...] + twin_aux[...]

    @pl.loop(1, chips)
    def _(step):
        other = lax.rem(chip + step, chips)
        remote(own_aux.at[sixteen(other)], aux.at[sixteen(chips - step)], 4, far(step))

    aux[pl.ds(0, PAIR), :] = own_aux[sixteen(chip), :]

    few = (parts - 1) * share
    await_bytes(weight_ref.at[pl.ds(0, few)], recv_sems.at[2])
    most = pl.ds(0, (chips - 1) * PAIR)
    await_bytes(rows.at[most], recv_sems.at[3])

    for j in range(0, parts, 2):
        two = dot(rows[...], wide[:, j * hidden : (j + 2) * hidden]).astype(BF16)
        partial[j] = two[:, :hidden]
        partial[j + 1] = two[:, hidden:]

    @pl.loop(1, parts)
    def _(step):
        other = lax.rem(part + step, parts)
        remote(partial.at[other], terms.at[part], 5, (other, place))

    terms[part] = partial[part]
    await_bytes(terms.at[pl.ds(0, parts - 1)], recv_sems.at[5])
    gate = terms[0].astype(F32)
    for i in range(1, parts):
        gate = gate + terms[i].astype(F32)
    await_bytes(aux.at[most], recv_sems.at[4])
    logistic = jax.nn.sigmoid(gate)
    slope = logistic * (1.0 + gate * (1.0 - logistic))
    delta[:, own_columns] = (aux[...].astype(F32) * slope).astype(BF16)

    @pl.loop(1, parts)
    def _(step):
        remote(delta.at[:, own_columns], delta.at[:, own_columns], 6, beside(step))

    await_bytes(terms.at[pl.ds(0, parts - 1)], recv_sems.at[6])
    back[...] = dot(delta[...], wide[...], ((1,), (1,))).astype(BF16)

    @pl.loop(1, chips)
    def _(step):
        remote(back.at[sixteen(step)], ret.at[sixteen(chip)], 7, far(step))

    ret[sixteen(chip), :] = back[pl.ds(0, PAIR), :]

    rows_turned = rows[...].T
    for j in range(0, parts, 2):
        two = dot(rows_turned, delta[:, j * hidden : (j + 2) * hidden]).astype(BF16)
        grads[j] = two[:share, :hidden]
        grads[j + 1] = two[:share, hidden:]

    own_share = pl.ds(pl.multiple_of(part * share, 16), share)

    @pl.loop(1, parts)
    def _(step):
        other = lax.rem(part + step, parts)
        remote(grads.at[other], weight_out.at[own_share], 8, (other, place))

    weight_out[own_share, :] = grads[part]

    await_bytes(ret.at[most], recv_sems.at[7])
    remote(ret, twin_ret, 9, twin)
    total = dot(pick[0], ret[...], ((0,), (0,)))
    await_bytes(twin_ret, recv_sems.at[9])
    total = total + dot(pick[1], twin_ret[...], ((0,), (0,)))
    token_out[...] = total[:, :share].astype(BF16)

    await_bytes(weight_out.at[pl.ds(0, few)], recv_sems.at[8])

    await_bytes(away_rows, send_sems.at[0])
    await_bytes(away_aux, send_sems.at[1])
    await_bytes(weight_ref.at[pl.ds(0, few)], send_sems.at[2])
    await_bytes(own_rows.at[most], send_sems.at[3])
    await_bytes(own_aux.at[most], send_sems.at[4])
    await_bytes(partial.at[pl.ds(0, parts - 1)], send_sems.at[5])
    await_bytes(partial.at[pl.ds(0, parts - 1)], send_sems.at[6])
    await_bytes(back.at[most], send_sems.at[7])
    await_bytes(weight_out.at[pl.ds(0, few)], send_sems.at[8])
    await_bytes(ret, send_sems.at[9])


def local(tokens, up_saved, hidden_grad, route_device, on_replica, gate_weight):
    experts = lax.axis_size("expert")
    parts = lax.axis_size("dp")
    part = lax.axis_index("dp")
    place = lax.axis_index("expert")
    chips = experts // 2
    tok_count, routes = route_device.shape
    width = tokens.shape[1]
    share = width // parts
    padded = -(-share // 128) * 128
    hidden = gate_weight.shape[2]
    slots = chips * PAIR
    tok = lax.dynamic_slice_in_dim(tokens, part * share, share, 1)
    tok = jnp.pad(tok, ((0, 0), (0, padded - share)))
    prod = (hidden_grad.astype(F32) * up_saved.astype(F32)).astype(BF16).transpose(1, 0, 2)
    flag = lax.dynamic_slice_in_dim(on_replica, place, 1, 0).reshape(experts, 1)
    vmem = pl.BlockSpec(memory_space=pltpu.VMEM)
    return pl.pallas_call(
        functools.partial(kernel, parts, chips, share),
        out_shape=(
            jax.ShapeDtypeStruct((tok_count, share), BF16),
            jax.ShapeDtypeStruct((width, hidden), BF16),
        ),
        in_specs=[vmem] * 5,
        out_specs=(vmem, vmem),
        scratch_shapes=[
            pltpu.VMEM((2, slots, tok_count), BF16),
            pltpu.VMEM((slots, padded), BF16),
            pltpu.VMEM((slots, hidden), BF16),
            pltpu.VMEM((slots, padded), BF16),
            pltpu.VMEM((slots, hidden), BF16),
            pltpu.VMEM((slots, padded), BF16),
            pltpu.VMEM((slots, hidden), BF16),
            pltpu.VMEM((slots, padded), BF16),
            pltpu.VMEM((slots, hidden), BF16),
            pltpu.VMEM((padded, parts * hidden), BF16),
            pltpu.VMEM((parts, slots, hidden), BF16),
            pltpu.VMEM((parts, slots, hidden), BF16),
            pltpu.VMEM((slots, parts * hidden), BF16),
            pltpu.VMEM((slots, padded), BF16),
            pltpu.VMEM((slots, padded), BF16),
            pltpu.VMEM((slots, padded), BF16),
            pltpu.VMEM((parts, share, hidden), BF16),
            pltpu.SemaphoreType.DMA((10,)),
            pltpu.SemaphoreType.DMA((10,)),
        ],
        compiler_params=pltpu.CompilerParams(
            collective_id=0, has_side_effects=True, vmem_limit_bytes=48 * 1024 * 1024
        ),
        cost_estimate=pl.CostEstimate(
            flops=6 * slots * padded * parts * hidden, bytes_accessed=4 << 20, transcendentals=0
        ),
    )(tok, prod, route_device.T, flag, gate_weight[0])


def solution(mesh):
    placed = (
        P("expert", None),
        P("expert", None, "dp"),
        P("expert", None, "dp"),
        P("expert", None),
        P(),
        P("expert", None, "dp"),
    )

    def whole(*args):
        token_grad, gate_grad = local(*args)
        return token_grad, gate_grad[None]

    return jax.shard_map(
        whole,
        mesh=mesh,
        in_specs=placed,
        out_specs=(P("expert", "dp"), P("expert", None, "dp")),
        check_vma=False,
    )
```

time: 721 us -> 159 us (0.22)
  waiting for transfers between devices: 579 us -> 0 us
  Pallas kernels: 0 us -> 154 us
  starting transfers between devices: 86.2 us -> 0 us
  other arithmetic: 21.5 us -> 1.11 us
  between operations: 14.3 us -> 0.7 us
  matrix products: 8.12 us -> 0 us
  local copies, waits for them, and re-layouts: 10.8 us -> 2.94 us
    reduce_scatter x1 -> x0, waiting for transfers between devices: 276 us -> none  [local(): lax.psum_scatter(partial_value.astype(jnp.bfloat16), 'dp', scatter_dimens...]
    all_to_all x3 -> x0, waiting for transfers between devices: 201 us -> none  [the longest x1 145 us: local(): lax.all_to_all(rows_send.reshape(experts, CAP, model_width), 'expert', sp...]
    pallas_call x0 -> x1, Pallas kernels: none -> 154 us  [local(): pl.pallas_call(functools.partial(kernel, parts, chips, share), out_shape=...]
    ppermute x2 -> x0, waiting for transfers between devices: 102 us -> none  [shifted(): lax.ppermute(value, axis, [(i, (i + by) % length) for i in range(length)])]
    all_to_all x3 -> x0, starting transfers between devices: 62.4 us -> none  [the longest x1 30.4 us: local(): lax.all_to_all(aux_send, 'expert', split_axis=0, concat_axis=0, tiled=True)]
    ppermute x2 -> x0, starting transfers between devices: 23.8 us -> none  [shifted(): lax.ppermute(value, axis, [(i, (i + by) % length) for i in range(length)])]
    another operation x3 -> x0, other arithmetic: 18.2 us -> none
    dot_general x6 -> x0, matrix products: 8.12 us -> none  [the longest x1 3.34 us: local(): jnp.einsum('sh,dh->sd', delta_both, both_weights, preferred_element_type=...]
  transfers between devices with their start and end apart: 6 -> 0, of which waited for: 5 -> 0; matrix products, arithmetic and copies ran while one was open for 2% -> 0% of each run, Pallas kernels for 0% -> 0%
where the time goes in v1:
time: 159 us
  Pallas kernels  154 us (97%)
  local copies, waits for them, and re-layouts  2.94 us (2%)
    pallas_call x1, Pallas kernels, local(): pl.pallas_call(functools.partial(kernel, parts, chips, share), out_shape=...  154 us

profile of v1, /device:TPU:1, one launch (start us, length us, event | category | flops | bytes accessed | tf_op | source)
XLA Modules:
  0.0 159.2 jit_solution(9795805702418337938)
XLA Ops:
  0.6 0.0 copy-start
  0.6 0.0 copy-start.1
  0.7 0.8 dynamic-slice_bitcast_fusion
  1.5 0.1 copy.10.flag_ref
  1.6 0.2 copy-done
  1.8 0.1 constant_dynamic-slice_fusion
  1.9 0.0 copy-start.2
  2.0 1.1 fusion.prod_ref
  3.1 0.0 copy-done.1
  3.1 0.0 copy-done.2
  3.1 154.5 %shard_map.77 = (bf16[128,224]{1,0:T(8,128)(2,1)S(1)}, bf16[3584,128]{1,0:T(8,128)(2,1)S(1)}) custom-call(bf16[128,256]{1,0:T(8,128)(2,1)S(1)} %pad.4.tok_ref, bf16[8,128,128]{2,1,0:T(8,128)(2,1)S(1)} %fusion.prod_ref, s32[8,128]{1,0:T(8,128)S(1)} %bitcast.9, s32[64,1]{1,0:T(8,128)S(1)} %copy.10.flag_ref, bf16[3584,128]{1,0:T(8,128)(2,1)S(1)} %bitcast.8), custom_call_target="tpu_custom_call" | custom-call | flops 1610612736 | bytes 4194304 | tf_op jit(solution)/shard_map/pallas_call | solution.py:276
  157.6 0.7 copy.11
  158.3 0.9 copy.15
  (1 shorter events, 0.0 us)
Async XLA Ops:
  0.6 1.2 copy-start
  0.6 2.4 %copy-start.1 = (bf16[1,3584,128]{2,1,0:T(8,128)(2,1)S(1)}, bf16[1,3584,128]{2,1,0:T(8,128)(2,1)}, u32[]{:S(2)}) copy-start(bf16[1,3584,128]{2,1,0:T(8,128)(2,1)} %param.11) | copy-start | bytes 2752516
  1.9 1.1 copy-start.2

commit v2 on v1

v2 whole, which is shorter than its diff:
```python
import functools
import math

import jax
import jax.numpy as jnp
from jax import lax
from jax.experimental import pallas as pl
from jax.experimental.pallas import tpu as pltpu
from jax.sharding import PartitionSpec as P

CAP = 4
SLOTS = 2 * CAP
PAIR = 2 * SLOTS
BATCHES = 4
MESH = pl.DeviceIdType.MESH
F32 = jnp.float32
BF16 = jnp.bfloat16


def dot(a, b, contract=((1,), (0,))):
    return lax.dot_general(a, b, (contract, ((), ())), preferred_element_type=F32)


def await_bytes(view, sem):
    pltpu.make_async_copy(view, view, sem).wait()


def kernel(
    parts,
    chips,
    share,
    tok_ref,
    prod_ref,
    route_ref,
    flag_ref,
    weight_ref,
    token_out,
    weight_out,
    pick,
    own_rows,
    own_aux,
    away_rows,
    away_aux,
    twin_rows,
    twin_aux,
    rows,
    aux,
    wide,
    partial,
    first_terms,
    half_sums,
    second_terms,
    delta,
    back,
    ret,
    twin_ret,
    totals,
    grads,
    send_sems,
    recv_sems,
):
    experts = 2 * chips
    halfway = experts // 2
    slots = chips * PAIR
    near = chips // BATCHES
    size = slots // BATCHES
    half = size // 2
    edge = half_sums.shape[2]
    tokens = tok_ref.shape[0]
    hidden = prod_ref.shape[2]
    routes = prod_ref.shape[0]
    part = lax.axis_index("dp")
    place = lax.axis_index("expert")
    line, spot = part // edge, part % edge
    chip = place // 2
    core = place % 2
    twin = (part, chip * 2 + 1 - core)
    first, second = pl.ds(0, half), pl.ds(half, half)

    def ahead(step):
        return (part, lax.rem(chip + step, chips) * 2 + core)

    def behind(step):
        return (part, lax.rem(chip + chips - step, chips) * 2 + core)

    def along(step):
        return lax.rem(spot + step, edge)

    def across(step):
        return lax.rem(line + step, edge)

    barrier = pltpu.get_barrier_semaphore()

    def greet(device):
        pl.semaphore_signal(barrier, inc=1, device_id=device, device_id_type=MESH)

    greet(twin)

    @pl.loop(1, chips)
    def _(step):
        greet(ahead(step))

    @pl.loop(1, parts)
    def _(step):
        greet((lax.rem(part + step, parts), place))

    wide[pl.ds(share, wide.shape[0] - share), :] = jnp.zeros(
        (wide.shape[0] - share, wide.shape[1]), BF16
    )

    named = route_ref[...]
    numbers = lax.broadcasted_iota(jnp.int32, (experts, tokens), 0)
    count = jnp.zeros((experts, tokens), F32)
    for k in range(routes):
        count = count + jnp.where(named[k : k + 1, :] == numbers, 1.0, 0.0)
    before = lax.broadcasted_iota(jnp.int32, (tokens, tokens), 0)
    after = lax.broadcasted_iota(jnp.int32, (tokens, tokens), 1)
    earlier = dot(count.astype(BF16), jnp.where(before < after, 1.0, 0.0).astype(BF16))
    flags = flag_ref[...].astype(F32)
    target = []
    for k in range(routes):
        here = named[k : k + 1, :] == numbers
        position = jnp.sum(jnp.where(here, earlier, 0.0), axis=0, keepdims=True).astype(jnp.int32)
        flag = jnp.sum(jnp.where(here, flags, 0.0), axis=0, keepdims=True).astype(jnp.int32)
        number = named[k : k + 1, :]
        server = lax.rem(number + flag * halfway, experts)
        step = lax.rem(chip + chips - server // 2, chips)
        order = lax.rem(step, BATCHES) * near + step // BATCHES
        row = order * PAIR + core * SLOTS + flag * CAP + position
        target.append((jnp.where(number < experts, row, -1), lax.rem(server, 2)))

    row_ids = lax.broadcasted_iota(jnp.int32, (slots, tokens), 0)

    def fill(side, rows_ref, aux_ref):
        total = jnp.zeros((slots, hidden), F32)
        every = jnp.zeros((slots, tokens), F32)
        for k in range(routes):
            row, parity = target[k]
            chosen = jnp.where(row_ids == jnp.where(parity == side, row, -1), 1.0, 0.0)
            every = every + chosen
            total = total + dot(chosen.astype(BF16), prod_ref[k])
        matrix = every.astype(BF16)
        rows_ref[...] = dot(matrix, tok_ref[...]).astype(BF16)
        aux_ref[...] = total.astype(BF16)
        return matrix

    pick[1] = fill(1 - core, away_rows, away_aux)
    pl.semaphore_wait(barrier, 1 + (chips - 1) + (parts - 1))

    def remote(src, dst, sem, device):
        copy = pltpu.make_async_remote_copy(
            src_ref=src,
            dst_ref=dst,
            send_sem=send_sems.at[sem],
            recv_sem=recv_sems.at[sem],
            device_id=device,
            device_id_type=MESH,
        )
        copy.start()

    twin_rows_sem, twin_aux_sem, weight_sem, grad_sem = range(4)
    rows_sem, aux_sem, first_sem, second_sem, third_sem, fourth_sem, ret_sem, twin_sem = (
        4 + BATCHES * i for i in range(8)
    )

    remote(away_rows, twin_rows, twin_rows_sem, twin)
    remote(away_aux, twin_aux, twin_aux_sem, twin)

    own_columns = pl.ds(pl.multiple_of(part * hidden, hidden), hidden)

    @pl.loop(1, parts)
    def _(step):
        other = lax.rem(part + step, parts)
        remote(
            weight_ref.at[pl.ds(pl.multiple_of(other * share, 16), share)],
            wide.at[pl.ds(0, share), own_columns],
            weight_sem,
            (other, place),
        )

    wide[pl.ds(0, share), own_columns] = weight_ref[
        pl.ds(pl.multiple_of(part * share, 16), share), :
    ]
    pick[0] = fill(core, own_rows, own_aux)

    def group(index):
        return pl.ds(pl.multiple_of(index * PAIR, PAIR), PAIR)

    def arrived(batch):
        lowest = batch * size + (PAIR if batch == 0 else 0)
        return pl.ds(lowest, (batch + 1) * size - lowest)

    def spread(batch, src, dst, sem, device_of):
        @pl.loop(1 if batch == 0 else 0, near)
        def _(index):
            where = group(batch * near + index)
            remote(src.at[where], dst.at[where], sem + batch, device_of(index * BATCHES + batch))

        if batch == 0:
            dst[pl.ds(0, PAIR), :] = src[pl.ds(0, PAIR), :]

    await_bytes(twin_rows, recv_sems.at[twin_rows_sem])
    own_rows[...] = own_rows[...] + twin_rows[...]
    spread(0, own_rows, rows, rows_sem, behind)
    await_bytes(twin_aux, recv_sems.at[twin_aux_sem])
    own_aux[...] = own_aux[...] + twin_aux[...]
    spread(0, own_aux, aux, aux_sem, behind)
    for batch in range(1, BATCHES):
        spread(batch, own_rows, rows, rows_sem, behind)
        spread(batch, own_aux, aux, aux_sem, behind)

    def batch_rows(batch):
        return rows[pl.ds(batch * size, size), :]

    def gate_terms(batch):
        await_bytes(rows.at[arrived(batch)], recv_sems.at[rows_sem + batch])
        for j in range(0, parts, 2):
            two = dot(batch_rows(batch), wide[:, j * hidden : (j + 2) * hidden]).astype(BF16)
            partial[batch, j // edge, j % edge] = two[:, :hidden]
            partial[batch, j // edge, j % edge + 1] = two[:, hidden:]

        @pl.loop(1, edge)
        def _(step):
            remote(
                partial.at[batch, :, along(step), first],
                first_terms.at[batch, 0, step - 1],
                first_sem + batch,
                (line * edge + along(step), place),
            )
            remote(
                partial.at[batch, across(step), :, second],
                first_terms.at[batch, 1, step - 1],
                first_sem + batch,
                (across(step) * edge + spot, place),
            )

    def gate_half_sums(batch):
        await_bytes(first_terms.at[batch], recv_sems.at[first_sem + batch])
        one = partial[batch, :, spot, first, :].astype(F32)
        two = partial[batch, line, :, second, :].astype(F32)
        for i in range(edge - 1):
            one = one + first_terms[batch, 0, i].astype(F32)
            two = two + first_terms[batch, 1, i].astype(F32)
        half_sums[batch, 0] = one.astype(BF16)
        half_sums[batch, 1] = two.astype(BF16)

        @pl.loop(1, edge)
        def _(step):
            remote(
                half_sums.at[batch, 0, across(step)],
                second_terms.at[batch, 0, step - 1],
                second_sem + batch,
                (across(step) * edge + spot, place),
            )
            remote(
                half_sums.at[batch, 1, along(step)],
                second_terms.at[batch, 1, step - 1],
                second_sem + batch,
                (line * edge + along(step), place),
            )

    def gate_delta(batch):
        await_bytes(second_terms.at[batch], recv_sems.at[second_sem + batch])
        await_bytes(aux.at[arrived(batch)], recv_sems.at[aux_sem + batch])
        for which, mine, there in ((0, line, first), (1, spot, second)):
            gate = half_sums[batch, which, mine].astype(F32)
            for i in range(edge - 1):
                gate = gate + second_terms[batch, which, i].astype(F32)
            logistic = jax.nn.sigmoid(gate)
            slope = logistic * (1.0 + gate * (1.0 - logistic))
            factor = aux[pl.ds(batch * size + which * half, half), :].astype(F32)
            delta[batch, line, spot, there, :] = (factor * slope).astype(BF16)

        @pl.loop(1, edge)
        def _(step):
            one = delta.at[batch, line, spot, first]
            remote(one, one, third_sem + batch, (across(step) * edge + spot, place))
            two = delta.at[batch, line, spot, second]
            remote(two, two, third_sem + batch, (line * edge + along(step), place))

    def pass_delta(batch):
        await_bytes(second_terms.at[batch], recv_sems.at[third_sem + batch])

        @pl.loop(1, edge)
        def _(step):
            one = delta.at[batch, :, spot, first]
            remote(one, one, fourth_sem + batch, (line * edge + along(step), place))
            two = delta.at[batch, line, :, second]
            remote(two, two, fourth_sem + batch, (across(step) * edge + spot, place))

    def two_parts(batch, j):
        row, column = j // edge, j % edge
        return jnp.concatenate(
            [delta[batch, row, column], delta[batch, row, column + 1]], axis=1
        )

    def route_grads(batch):
        await_bytes(first_terms.at[batch], recv_sems.at[fourth_sem + batch])
        total = jnp.zeros((size, wide.shape[0]), F32)
        for j in range(0, parts, 2):
            columns = wide[:, j * hidden : (j + 2) * hidden]
            total = total + dot(two_parts(batch, j), columns, ((1,), (1,)))
        back[pl.ds(batch * size, size), :] = total.astype(BF16)
        spread(batch, back, ret, ret_sem, ahead)

    def weight_grads(batch):
        turned = batch_rows(batch).T
        for j in range(0, parts, 2):
            there = slice(j * hidden, (j + 2) * hidden)
            two = dot(turned, two_parts(batch, j))
            if batch > 0:
                two = two + totals[:, there]
            if batch < BATCHES - 1:
                totals[:, there] = two
            else:
                grads[j] = two[:share, :hidden].astype(BF16)
                grads[j + 1] = two[:share, hidden:].astype(BF16)

    few = (parts - 1) * share
    await_bytes(weight_ref.at[pl.ds(0, few)], recv_sems.at[weight_sem])
    for batch in range(BATCHES):
        gate_terms(batch)
        if batch > 0:
            pass_delta(batch - 1)
        gate_half_sums(batch)
        if batch > 0:
            route_grads(batch - 1)
            weight_grads(batch - 1)
        gate_delta(batch)
    last = BATCHES - 1
    pass_delta(last)
    route_grads(last)
    weight_grads(last)

    own_share = pl.ds(pl.multiple_of(part * share, 16), share)

    @pl.loop(1, parts)
    def _(step):
        other = lax.rem(part + step, parts)
        remote(grads.at[other], weight_out.at[own_share], grad_sem, (other, place))

    weight_out[own_share, :] = grads[part]

    def hand_over(batch):
        there = pl.ds(batch * size, size)
        await_bytes(ret.at[arrived(batch)], recv_sems.at[ret_sem + batch])
        remote(ret.at[there], twin_ret.at[there], twin_sem + batch, twin)

    for batch in range(BATCHES):
        hand_over(batch)
    total = dot(pick[0], ret[...], ((0,), (0,)))
    for batch in range(BATCHES):
        await_bytes(twin_ret.at[pl.ds(batch * size, size)], recv_sems.at[twin_sem + batch])
    total = total + dot(pick[1], twin_ret[...], ((0,), (0,)))
    token_out[...] = total[:, :share].astype(BF16)

    await_bytes(away_rows, send_sems.at[twin_rows_sem])
    await_bytes(away_aux, send_sems.at[twin_aux_sem])
    await_bytes(weight_ref.at[pl.ds(0, few)], send_sems.at[weight_sem])
    for batch in range(BATCHES):
        await_bytes(rows.at[arrived(batch)], send_sems.at[rows_sem + batch])
        await_bytes(aux.at[arrived(batch)], send_sems.at[aux_sem + batch])
        await_bytes(first_terms.at[batch], send_sems.at[first_sem + batch])
        await_bytes(second_terms.at[batch], send_sems.at[second_sem + batch])
        await_bytes(second_terms.at[batch], send_sems.at[third_sem + batch])
        await_bytes(first_terms.at[batch], send_sems.at[fourth_sem + batch])
        await_bytes(back.at[arrived(batch)], send_sems.at[ret_sem + batch])
        await_bytes(ret.at[pl.ds(batch * size, size)], send_sems.at[twin_sem + batch])
    await_bytes(weight_out.at[pl.ds(0, few)], send_sems.at[grad_sem])
    await_bytes(weight_out.at[pl.ds(0, few)], recv_sems.at[grad_sem])


def local(tokens, up_saved, hidden_grad, route_device, on_replica, gate_weight):
    experts = lax.axis_size("expert")
    parts = lax.axis_size("dp")
    part = lax.axis_index("dp")
    place = lax.axis_index("expert")
    chips = experts // 2
    tok_count, routes = route_device.shape
    width = tokens.shape[1]
    share = width // parts
    padded = -(-share // 128) * 128
    hidden = gate_weight.shape[2]
    slots = chips * PAIR
    size = slots // BATCHES
    edge = math.isqrt(parts)
    tok = lax.dynamic_slice_in_dim(tokens, part * share, share, 1)
    tok = jnp.pad(tok, ((0, 0), (0, padded - share)))
    prod = (hidden_grad.astype(F32) * up_saved.astype(F32)).astype(BF16).transpose(1, 0, 2)
    flag = lax.dynamic_slice_in_dim(on_replica, place, 1, 0).reshape(experts, 1)
    vmem = pl.BlockSpec(memory_space=pltpu.VMEM)
    return pl.pallas_call(
        functools.partial(kernel, parts, chips, share),
        out_shape=(
            jax.ShapeDtypeStruct((tok_count, share), BF16),
            jax.ShapeDtypeStruct((width, hidden), BF16),
        ),
        in_specs=[vmem] * 5,
        out_specs=(vmem, vmem),
        scratch_shapes=[
            pltpu.VMEM((2, slots, tok_count), BF16),
            pltpu.VMEM((slots, padded), BF16),
            pltpu.VMEM((slots, hidden), BF16),
            pltpu.VMEM((slots, padded), BF16),
            pltpu.VMEM((slots, hidden), BF16),
            pltpu.VMEM((slots, padded), BF16),
            pltpu.VMEM((slots, hidden), BF16),
            pltpu.VMEM((slots, padded), BF16),
            pltpu.VMEM((slots, hidden), BF16),
            pltpu.VMEM((padded, parts * hidden), BF16),
            pltpu.VMEM((BATCHES, edge, edge, size, hidden), BF16),
            pltpu.VMEM((BATCHES, 2, edge - 1, edge, size // 2, hidden), BF16),
            pltpu.VMEM((BATCHES, 2, edge, size // 2, hidden), BF16),
            pltpu.VMEM((BATCHES, 2, edge - 1, size // 2, hidden), BF16),
            pltpu.VMEM((BATCHES, edge, edge, size, hidden), BF16),
            pltpu.VMEM((slots, padded), BF16),
            pltpu.VMEM((slots, padded), BF16),
            pltpu.VMEM((slots, padded), BF16),
            pltpu.VMEM((padded, parts * hidden), F32),
            pltpu.VMEM((parts, share, hidden), BF16),
            pltpu.SemaphoreType.DMA((4 + 8 * BATCHES,)),
            pltpu.SemaphoreType.DMA((4 + 8 * BATCHES,)),
        ],
        compiler_params=pltpu.CompilerParams(
            collective_id=0, has_side_effects=True, vmem_limit_bytes=48 * 1024 * 1024
        ),
        cost_estimate=pl.CostEstimate(
            flops=6 * slots * padded * parts * hidden, bytes_accessed=4 << 20, transcendentals=0
        ),
    )(tok, prod, route_device.T, flag, gate_weight[0])


def solution(mesh):
    placed = (
        P("expert", None),
        P("expert", None, "dp"),
        P("expert", None, "dp"),
        P("expert", None),
        P(),
        P("expert", None, "dp"),
    )

    def whole(*args):
        token_grad, gate_grad = local(*args)
        return token_grad, gate_grad[None]

    return jax.shard_map(
        whole,
        mesh=mesh,
        in_specs=placed,
        out_specs=(P("expert", "dp"), P("expert", None, "dp")),
        check_vma=False,
    )
```

time: 159 us -> 118 us (0.74)
  Pallas kernels: 154 us -> 113 us
    pallas_call x1, Pallas kernels: 154 us -> 113 us  [local(): pl.pallas_call(functools.partial(kernel, parts, chips, share), out_shape=...]
where the time goes in v2:
time: 118 us
  Pallas kernels  113 us (96%)
  local copies, waits for them, and re-layouts  2.94 us (2%)
    pallas_call x1, Pallas kernels, local(): pl.pallas_call(functools.partial(kernel, parts, chips, share), out_shape=...  113 us

profile of v2, /device:TPU:1, one launch (start us, length us, event | category | flops | bytes accessed | tf_op | source)
XLA Modules:
  0.0 118.2 jit_solution(13292934966398544941)
XLA Ops:
  0.6 0.0 copy-start
  0.6 0.0 copy-start.1
  0.7 0.8 dynamic-slice_bitcast_fusion
  1.5 0.1 copy.10.flag_ref
  1.6 0.2 copy-done
  1.8 0.1 constant_dynamic-slice_fusion
  1.9 0.0 copy-start.2
  2.0 1.1 fusion.prod_ref
  3.1 0.0 copy-done.1
  3.1 0.0 copy-done.2
  3.1 113.4 %shard_map.77 = (bf16[128,224]{1,0:T(8,128)(2,1)S(1)}, bf16[3584,128]{1,0:T(8,128)(2,1)S(1)}) custom-call(bf16[128,256]{1,0:T(8,128)(2,1)S(1)} %pad.4.tok_ref, bf16[8,128,128]{2,1,0:T(8,128)(2,1)S(1)} %fusion.prod_ref, s32[8,128]{1,0:T(8,128)S(1)} %bitcast.9, s32[64,1]{1,0:T(8,128)S(1)} %copy.10.flag_ref, bf16[3584,128]{1,0:T(8,128)(2,1)S(1)} %bitcast.8), custom_call_target="tpu_custom_call" | custom-call | flops 1610612736 | bytes 4194304 | tf_op jit(solution)/shard_map/pallas_call | solution.py:392
  116.5 0.7 copy.11
  117.2 0.9 copy.15
  (1 shorter events, 0.0 us)
Async XLA Ops:
  0.6 1.2 %copy-start = (bf16[128,3584]{1,0:T(8,128)(2,1)S(1)}, bf16[128,3584]{1,0:T(8,128)(2,1)}, u32[]{:S(2)}) copy-start(bf16[128,3584]{1,0:T(8,128)(2,1)} %param.6) | copy-start | bytes 2752516
  0.6 2.4 %copy-start.1 = (bf16[1,3584,128]{2,1,0:T(8,128)(2,1)S(1)}, bf16[1,3584,128]{2,1,0:T(8,128)(2,1)}, u32[]{:S(2)}) copy-start(bf16[1,3584,128]{2,1,0:T(8,128)(2,1)} %param.11) | copy-start | bytes 2752516
  1.9 1.1 copy-start.2

commit v3 on v2

--- a/solution.py
+++ b/solution.py
@@ -12,6 +12,14 @@
 SLOTS = 2 * CAP
 PAIR = 2 * SLOTS
 BATCHES = 4
+SENDS = (
+    "r0", "a0", "r3", "r2", "a3", "r1", "a2", "a1",
+)
+ORDER = (
+    "a0", "b0", "c0", "d0", "a3", "a2", "b3", "e0", "a1", "b2",
+    "c3", "b1", "d3", "c2", "e3", "d2", "c1", "e2", "d1", "e1",
+)
+SEQUENCE = [int(step[1:]) for step in ORDER if step[0] == "e"]
 MESH = pl.DeviceIdType.MESH
 F32 = jnp.float32
 BF16 = jnp.bfloat16
@@ -78,7 +86,7 @@
     first, second = pl.ds(0, half), pl.ds(half, half)
 
     def ahead(step):
-        return (part, lax.rem(chip + step, chips) * 2 + core)
+        return (part, lax.rem(chip + chips + step, chips) * 2 + core)
 
     def behind(step):
         return (part, lax.rem(chip + chips - step, chips) * 2 + core)
@@ -94,15 +102,18 @@
     def greet(device):
         pl.semaphore_signal(barrier, inc=1, device_id=device, device_id_type=MESH)
 
-    greet(twin)
-
-    @pl.loop(1, chips)
+    greet(ahead(chips // 2))
+
+    @pl.loop(1, chips // 2)
     def _(step):
-        greet(ahead(step))
+        greet(ahead(chips // 2 - step))
+        greet(behind(chips // 2 - step))
 
     @pl.loop(1, parts)
     def _(step):
         greet((lax.rem(part + step, parts), place))
+
+    greet(twin)
 
     wide[pl.ds(share, wide.shape[0] - share), :] = jnp.zeros(
         (wide.shape[0] - share, wide.shape[1]), BF16
@@ -124,9 +135,9 @@
         flag = jnp.sum(jnp.where(here, flags, 0.0), axis=0, keepdims=True).astype(jnp.int32)
         number = named[k : k + 1, :]
         server = lax.rem(number + flag * halfway, experts)
-        step = lax.rem(chip + chips - server // 2, chips)
-        order = lax.rem(step, BATCHES) * near + step // BATCHES
-        row = order * PAIR + core * SLOTS + flag * CAP + position
+        offset = lax.rem(chip + chips + chips // 2 - server // 2, chips) - chips // 2
+        rank = jnp.where(offset < 0, -2 * offset - 1, 2 * offset)
+        row = rank * PAIR + core * SLOTS + flag * CAP + position
         target.append((jnp.where(number < experts, row, -1), lax.rem(server, 2)))
 
     row_ids = lax.broadcasted_iota(jnp.int32, (slots, tokens), 0)
@@ -145,6 +156,7 @@
         return matrix
 
     pick[1] = fill(1 - core, away_rows, away_aux)
+    pick[0] = fill(core, own_rows, own_aux)
     pl.semaphore_wait(barrier, 1 + (chips - 1) + (parts - 1))
 
     def remote(src, dst, sem, device):
@@ -181,7 +193,6 @@
     wide[pl.ds(0, share), own_columns] = weight_ref[
         pl.ds(pl.multiple_of(part * share, 16), share), :
     ]
-    pick[0] = fill(core, own_rows, own_aux)
 
     def group(index):
         return pl.ds(pl.multiple_of(index * PAIR, PAIR), PAIR)
@@ -191,22 +202,28 @@
         return pl.ds(lowest, (batch + 1) * size - lowest)
 
     def spread(batch, src, dst, sem, device_of):
-        @pl.loop(1 if batch == 0 else 0, near)
+        @pl.loop(0, near - 1 if batch == 0 else near, unroll=True)
         def _(index):
-            where = group(batch * near + index)
-            remote(src.at[where], dst.at[where], sem + batch, device_of(index * BATCHES + batch))
+            rank = (batch + 1) * near - 1 - index
+            offset = jnp.where(lax.rem(rank, 2) == 1, -((rank + 1) // 2), rank // 2)
+            where = group(rank)
+            remote(src.at[where], dst.at[where], sem + batch, device_of(offset))
 
         if batch == 0:
             dst[pl.ds(0, PAIR), :] = src[pl.ds(0, PAIR), :]
 
     await_bytes(twin_rows, recv_sems.at[twin_rows_sem])
     own_rows[...] = own_rows[...] + twin_rows[...]
-    spread(0, own_rows, rows, rows_sem, behind)
-    await_bytes(twin_aux, recv_sems.at[twin_aux_sem])
-    own_aux[...] = own_aux[...] + twin_aux[...]
-    spread(0, own_aux, aux, aux_sem, behind)
-    for batch in range(1, BATCHES):
-        spread(batch, own_rows, rows, rows_sem, behind)
+    added = False
+    for item in SENDS:
+        batch = int(item[1:])
+        if item[0] == "r":
+            spread(batch, own_rows, rows, rows_sem, behind)
+            continue
+        if not added:
+            await_bytes(twin_aux, recv_sems.at[twin_aux_sem])
+            own_aux[...] = own_aux[...] + twin_aux[...]
+            added = True
         spread(batch, own_aux, aux, aux_sem, behind)
 
     def batch_rows(batch):
@@ -219,7 +236,7 @@
             partial[batch, j // edge, j % edge] = two[:, :hidden]
             partial[batch, j // edge, j % edge + 1] = two[:, hidden:]
 
-        @pl.loop(1, edge)
+        @pl.loop(1, edge, unroll=True)
         def _(step):
             remote(
                 partial.at[batch, :, along(step), first],
@@ -244,7 +261,7 @@
         half_sums[batch, 0] = one.astype(BF16)
         half_sums[batch, 1] = two.astype(BF16)
 
-        @pl.loop(1, edge)
+        @pl.loop(1, edge, unroll=True)
         def _(step):
             remote(
                 half_sums.at[batch, 0, across(step)],
@@ -271,7 +288,7 @@
             factor = aux[pl.ds(batch * size + which * half, half), :].astype(F32)
             delta[batch, line, spot, there, :] = (factor * slope).astype(BF16)
 
-        @pl.loop(1, edge)
+        @pl.loop(1, edge, unroll=True)
         def _(step):
             one = delta.at[batch, line, spot, first]
             remote(one, one, third_sem + batch, (across(step) * edge + spot, place))
@@ -281,7 +298,7 @@
     def pass_delta(batch):
         await_bytes(second_terms.at[batch], recv_sems.at[third_sem + batch])
 
-        @pl.loop(1, edge)
+        @pl.loop(1, edge, unroll=True)
         def _(step):
             one = delta.at[batch, :, spot, first]
             remote(one, one, fourth_sem + batch, (line * edge + along(step), place))
@@ -295,7 +312,6 @@
         )
 
     def route_grads(batch):
-        await_bytes(first_terms.at[batch], recv_sems.at[fourth_sem + batch])
         total = jnp.zeros((size, wide.shape[0]), F32)
         for j in range(0, parts, 2):
             columns = wide[:, j * hidden : (j + 2) * hidden]
@@ -308,9 +324,9 @@
         for j in range(0, parts, 2):
             there = slice(j * hidden, (j + 2) * hidden)
             two = dot(turned, two_parts(batch, j))
-            if batch > 0:
+            if batch != SEQUENCE[0]:
                 two = two + totals[:, there]
-            if batch < BATCHES - 1:
+            if batch != SEQUENCE[-1]:
                 totals[:, there] = two
             else:
                 grads[j] = two[:share, :hidden].astype(BF16)
@@ -318,35 +334,36 @@
 
     few = (parts - 1) * share
     await_bytes(weight_ref.at[pl.ds(0, few)], recv_sems.at[weight_sem])
-    for batch in range(BATCHES):
-        gate_terms(batch)
-        if batch > 0:
-            pass_delta(batch - 1)
-        gate_half_sums(batch)
-        if batch > 0:
-            route_grads(batch - 1)
-            weight_grads(batch - 1)
-        gate_delta(batch)
-    last = BATCHES - 1
-    pass_delta(last)
-    route_grads(last)
-    weight_grads(last)
-
     own_share = pl.ds(pl.multiple_of(part * share, 16), share)
 
-    @pl.loop(1, parts)
-    def _(step):
-        other = lax.rem(part + step, parts)
-        remote(grads.at[other], weight_out.at[own_share], grad_sem, (other, place))
-
-    weight_out[own_share, :] = grads[part]
+    def send_weight_grads():
+        @pl.loop(1, parts)
+        def _(step):
+            other = lax.rem(part + step, parts)
+            remote(grads.at[other], weight_out.at[own_share], grad_sem, (other, place))
+
+        weight_out[own_share, :] = grads[part]
+
+    def close(batch):
+        await_bytes(first_terms.at[batch], recv_sems.at[fourth_sem + batch])
+        if batch == SEQUENCE[-1]:
+            weight_grads(batch)
+            send_weight_grads()
+            route_grads(batch)
+        else:
+            route_grads(batch)
+            weight_grads(batch)
+
+    stages = dict(a=gate_terms, b=gate_half_sums, c=gate_delta, d=pass_delta, e=close)
+    for step in ORDER:
+        stages[step[0]](int(step[1:]))
 
     def hand_over(batch):
         there = pl.ds(batch * size, size)
         await_bytes(ret.at[arrived(batch)], recv_sems.at[ret_sem + batch])
         remote(ret.at[there], twin_ret.at[there], twin_sem + batch, twin)
 
-    for batch in range(BATCHES):
+    for batch in SEQUENCE:
         hand_over(batch)
     total = dot(pick[0], ret[...], ((0,), (0,)))
     for batch in range(BATCHES):

time: 118 us -> 111 us (0.941)
  Pallas kernels: 113 us -> 106 us
    pallas_call x1, Pallas kernels: 113 us -> 106 us  [local(): pl.pallas_call(functools.partial(kernel, parts, chips, share), out_shape=...]
where the time goes in v3:
time: 111 us
  Pallas kernels  106 us (95%)
  local copies, waits for them, and re-layouts  2.94 us (3%)
  other arithmetic  1.11 us (1%)
    pallas_call x1, Pallas kernels, local(): pl.pallas_call(functools.partial(kernel, parts, chips, share), out_shape=...  106 us

profile of v3, /device:TPU:1, one launch (start us, length us, event | category | flops | bytes accessed | tf_op | source)
XLA Modules:
  0.0 110.6 jit_solution(5645611031719805805)
XLA Ops:
  0.6 0.0 copy-start
  0.6 0.0 copy-start.1
  0.7 0.8 dynamic-slice_bitcast_fusion
  1.5 0.1 copy.10.flag_ref
  1.6 0.2 copy-done
  1.8 0.1 constant_dynamic-slice_fusion
  1.9 0.0 copy-start.2
  2.0 1.1 %fusion.prod_ref = bf16[8,128,128]{2,1,0:T(8,128)(2,1)S(1)} fusion(bf16[128,8,128]{2,1,0:T(8,128)(2,1)} %param.7, bf16[128,8,128]{2,1,0:T(8,128)(2,1)} %param.8), kind=kLoop, calls=%fused_computation.1 | loop fusion | flops 524288 | bytes 786432 | tf_op jit(solution)/shard_map/transpose | solution.py:406
  3.1 0.0 copy-done.1
  3.1 0.0 copy-done.2
  3.1 105.8 %shard_map.77 = (bf16[128,224]{1,0:T(8,128)(2,1)S(1)}, bf16[3584,128]{1,0:T(8,128)(2,1)S(1)}) custom-call(bf16[128,256]{1,0:T(8,128)(2,1)S(1)} %pad.4.tok_ref, bf16[8,128,128]{2,1,0:T(8,128)(2,1)S(1)} %fusion.prod_ref, s32[8,128]{1,0:T(8,128)S(1)} %bitcast.9, s32[64,1]{1,0:T(8,128)S(1)} %copy.10.flag_ref, bf16[3584,128]{1,0:T(8,128)(2,1)S(1)} %bitcast.8), custom_call_target="tpu_custom_call" | custom-call | flops 1610612736 | bytes 4194304 | tf_op jit(solution)/shard_map/pallas_call | solution.py:409
  108.9 0.7 copy.11
  109.6 0.9 copy.15
  (1 shorter events, 0.0 us)
Async XLA Ops:
  0.6 1.2 %copy-start = (bf16[128,3584]{1,0:T(8,128)(2,1)S(1)}, bf16[128,3584]{1,0:T(8,128)(2,1)}, u32[]{:S(2)}) copy-start(bf16[128,3584]{1,0:T(8,128)(2,1)} %param.6) | copy-start | bytes 2752516
  0.6 2.4 %copy-start.1 = (bf16[1,3584,128]{2,1,0:T(8,128)(2,1)S(1)}, bf16[1,3584,128]{2,1,0:T(8,128)(2,1)}, u32[]{:S(2)}) copy-start(bf16[1,3584,128]{2,1,0:T(8,128)(2,1)} %param.11) | copy-start | bytes 2752516
  1.9 1.1 %copy-start.2 = (s32[128,8]{0,1:T(8,128)S(1)}, s32[128,8]{0,1:T(8,128)}, u32[]{:S(2)}) copy-start(s32[128,8]{0,1:T(8,128)} %param.9) | copy-start | bytes 12292

commit v4 on v3

--- a/solution.py
+++ b/solution.py
@@ -16,8 +16,8 @@
     "r0", "a0", "r3", "r2", "a3", "r1", "a2", "a1",
 )
 ORDER = (
-    "a0", "b0", "c0", "d0", "a3", "a2", "b3", "e0", "a1", "b2",
-    "c3", "b1", "d3", "c2", "e3", "d2", "c1", "e2", "d1", "e1",
+    "a0", "b0", "c0", "a3", "d0", "a2", "b3", "e0", "w0", "a1", "b2",
+    "c3", "b1", "d3", "c2", "c1", "d2", "e3", "d1", "w3", "e2", "w2", "e1",
 )
 SEQUENCE = [int(step[1:]) for step in ORDER if step[0] == "e"]
 MESH = pl.DeviceIdType.MESH
@@ -104,12 +104,12 @@
 
     greet(ahead(chips // 2))
 
-    @pl.loop(1, chips // 2)
+    @pl.loop(1, chips // 2, unroll=True)
     def _(step):
         greet(ahead(chips // 2 - step))
         greet(behind(chips // 2 - step))
 
-    @pl.loop(1, parts)
+    @pl.loop(1, parts, unroll=True)
     def _(step):
         greet((lax.rem(part + step, parts), place))
 
@@ -156,7 +156,6 @@
         return matrix
 
     pick[1] = fill(1 - core, away_rows, away_aux)
-    pick[0] = fill(core, own_rows, own_aux)
     pl.semaphore_wait(barrier, 1 + (chips - 1) + (parts - 1))
 
     def remote(src, dst, sem, device):
@@ -193,6 +192,8 @@
     wide[pl.ds(0, share), own_columns] = weight_ref[
         pl.ds(pl.multiple_of(part * share, 16), share), :
     ]
+
+    pick[0] = fill(core, own_rows, own_aux)
 
     def group(index):
         return pl.ds(pl.multiple_of(index * PAIR, PAIR), PAIR)
@@ -319,42 +320,42 @@
         back[pl.ds(batch * size, size), :] = total.astype(BF16)
         spread(batch, back, ret, ret_sem, ahead)
 
+    own_share = pl.ds(pl.multiple_of(part * share, 16), share)
+
     def weight_grads(batch):
         turned = batch_rows(batch).T
         for j in range(0, parts, 2):
             there = slice(j * hidden, (j + 2) * hidden)
             two = dot(turned, two_parts(batch, j))
-            if batch != SEQUENCE[0]:
-                two = two + totals[:, there]
-            if batch != SEQUENCE[-1]:
-                totals[:, there] = two
-            else:
-                grads[j] = two[:share, :hidden].astype(BF16)
-                grads[j + 1] = two[:share, hidden:].astype(BF16)
+            totals[:, there] = two if batch == SEQUENCE[0] else two + totals[:, there]
+
+    def last_weight_grads(batch):
+        turned = batch_rows(batch).T
+
+        @pl.loop(0, parts // 2)
+        def _(step):
+            j = 2 * lax.rem(part // 2 + step, parts // 2)
+            there = pl.ds(pl.multiple_of(j * hidden, 2 * hidden), 2 * hidden)
+            two = dot(turned, two_parts(batch, j)) + totals[:, there]
+            grads[j] = two[:share, :hidden].astype(BF16)
+            grads[j + 1] = two[:share, hidden:].astype(BF16)
+            for i in range(2):
+
+                @pl.when(j + i != part)
+                def _(other=j + i):
+                    remote(grads.at[other], weight_out.at[own_share], grad_sem, (other, place))
+
+        weight_out[own_share, :] = grads[part]
+
+    def finish(batch):
+        await_bytes(first_terms.at[batch], recv_sems.at[fourth_sem + batch])
+        if batch == SEQUENCE[-1]:
+            last_weight_grads(batch)
+        route_grads(batch)
 
     few = (parts - 1) * share
     await_bytes(weight_ref.at[pl.ds(0, few)], recv_sems.at[weight_sem])
-    own_share = pl.ds(pl.multiple_of(part * share, 16), share)
-
-    def send_weight_grads():
-        @pl.loop(1, parts)
-        def _(step):
-            other = lax.rem(part + step, parts)
-            remote(grads.at[other], weight_out.at[own_share], grad_sem, (other, place))
-
-        weight_out[own_share, :] = grads[part]
-
-    def close(batch):
-        await_bytes(first_terms.at[batch], recv_sems.at[fourth_sem + batch])
-        if batch == SEQUENCE[-1]:
-            weight_grads(batch)
-            send_weight_grads()
-            route_grads(batch)
-        else:
-            route_grads(batch)
-            weight_grads(batch)
-
-    stages = dict(a=gate_terms, b=gate_half_sums, c=gate_delta, d=pass_delta, e=close)
+    stages = dict(a=gate_terms, b=gate_half_sums, c=gate_delta, d=pass_delta, e=finish, w=weight_grads)
     for step in ORDER:
         stages[step[0]](int(step[1:]))
 
@@ -365,11 +366,11 @@
 
     for batch in SEQUENCE:
         hand_over(batch)
-    total = dot(pick[0], ret[...], ((0,), (0,)))
+    total = dot(ret[...], pick[0], ((0,), (0,)))
     for batch in range(BATCHES):
         await_bytes(twin_ret.at[pl.ds(batch * size, size)], recv_sems.at[twin_sem + batch])
-    total = total + dot(pick[1], twin_ret[...], ((0,), (0,)))
-    token_out[...] = total[:, :share].astype(BF16)
+    total = total + dot(twin_ret[...], pick[1], ((0,), (0,)))
+    token_out[...] = total[:share].astype(BF16)
 
     await_bytes(away_rows, send_sems.at[twin_rows_sem])
     await_bytes(away_aux, send_sems.at[twin_aux_sem])
@@ -409,7 +410,7 @@
     return pl.pallas_call(
         functools.partial(kernel, parts, chips, share),
         out_shape=(
-            jax.ShapeDtypeStruct((tok_count, share), BF16),
+            jax.ShapeDtypeStruct((share, tok_count), BF16),
             jax.ShapeDtypeStruct((width, hidden), BF16),
         ),
         in_specs=[vmem] * 5,
@@ -459,7 +460,7 @@
 
     def whole(*args):
         token_grad, gate_grad = local(*args)
-        return token_grad, gate_grad[None]
+        return token_grad.T, gate_grad[None]
 
     return jax.shard_map(
         whole,

time: 111 us -> 110 us (level)
  no operation moved by 1% of the time
where the time goes in v4:
time: 110 us
  Pallas kernels  106 us (96%)
  local copies, waits for them, and re-layouts  2.84 us (3%)
  other arithmetic  1.11 us (1%)
    pallas_call x1, Pallas kernels, local(): pl.pallas_call(functools.partial(kernel, parts, chips, share), out_shape=...  106 us

profile of v4, /device:TPU:1, one launch (start us, length us, event | category | flops | bytes accessed | tf_op | source)
XLA Modules:
  0.0 110.2 jit_solution(7725021488364596906)
XLA Ops:
  0.6 0.0 copy-start
  0.6 0.0 copy-start.1
  0.7 0.8 dynamic-slice_bitcast_fusion
  1.5 0.1 copy.10.flag_ref
  1.6 0.2 copy-done
  1.8 0.1 constant_dynamic-slice_fusion
  1.9 0.0 copy-start.2
  2.0 1.1 %fusion.prod_ref = bf16[8,128,128]{2,1,0:T(8,128)(2,1)S(1)} fusion(bf16[128,8,128]{2,1,0:T(8,128)(2,1)} %param.7, bf16[128,8,128]{2,1,0:T(8,128)(2,1)} %param.8), kind=kLoop, calls=%fused_computation.1 | loop fusion | flops 524288 | bytes 786432 | tf_op jit(solution)/shard_map/transpose | solution.py:407
  3.1 0.0 copy-done.1
  3.1 0.0 copy-done.2
  3.1 105.5 %shard_map.77 = (bf16[224,128]{1,0:T(8,128)(2,1)S(1)}, bf16[3584,128]{1,0:T(8,128)(2,1)S(1)}) custom-call(bf16[128,256]{1,0:T(8,128)(2,1)S(1)} %pad.4.tok_ref, bf16[8,128,128]{2,1,0:T(8,128)(2,1)S(1)} %fusion.prod_ref, s32[8,128]{1,0:T(8,128)S(1)} %bitcast.11, s32[64,1]{1,0:T(8,128)S(1)} %copy.10.flag_ref, bf16[3584,128]{1,0:T(8,128)(2,1)S(1)} %bitcast.10), custom_call_target="tpu_custom_call" | custom-call | flops 1610612736 | bytes 4194304 | tf_op jit(solution)/shard_map/pallas_call | solution.py:410
  108.6 0.6 copy.15
  109.2 0.9 copy.16
  (1 shorter events, 0.0 us)
Async XLA Ops:
  0.6 1.2 %copy-start = (bf16[128,3584]{1,0:T(8,128)(2,1)S(1)}, bf16[128,3584]{1,0:T(8,128)(2,1)}, u32[]{:S(2)}) copy-start(bf16[128,3584]{1,0:T(8,128)(2,1)} %param.6) | copy-start | bytes 2752516
  0.6 2.4 %copy-start.1 = (bf16[1,3584,128]{2,1,0:T(8,128)(2,1)S(1)}, bf16[1,3584,128]{2,1,0:T(8,128)(2,1)}, u32[]{:S(2)}) copy-start(bf16[1,3584,128]{2,1,0:T(8,128)(2,1)} %param.11) | copy-start | bytes 2752516
  1.9 1.1 %copy-start.2 = (s32[128,8]{0,1:T(8,128)S(1)}, s32[128,8]{0,1:T(8,128)}, u32[]{:S(2)}) copy-start(s32[128,8]{0,1:T(8,128)} %param.9) | copy-start | bytes 12292
